TPU v7x, 32 devices: a whole 2x2x4 slice. The times are simulated.
32 devices in a mesh: fsdp: 8 (over z, y), dp: 4 (over x, core).
Axes of the slice: x: 2, y: 2, z: 4, core: 2. Of those that a mesh axis runs over, the one named last changes fastest.
Arguments:
- tokens: bfloat16 [4096, 4096], P(('fsdp', 'dp')), may hold values from -6 to 6
- gain: float32 [4096], replicated, may hold values from 0.5 to 1.5
- tiles: bfloat16 [128, 128, 128], P('fsdp'), may hold values from -0.5 to 0.5
- tile_rows: int32 [128], replicated, may hold values from 0 to 31, as said below
- tile_cols: int32 [128], replicated, may hold values from 0 to 111, as said below
- cotangent: bfloat16 [4096, 14336], P(('fsdp', 'dp')), may hold values from -6 to 6
Outputs:
- projected: bfloat16 [4096, 14336], P(('fsdp', 'dp'))
- token_grad: bfloat16 [4096, 4096], P(('fsdp', 'dp'))
- tile_grad: float32 [128, 128, 128], P('fsdp')
- gain_grad: float32 [4096], replicated
Inputs may be any that keep to these rules, and one draw needn't show every extreme that they name: The pairs (tile_rows[i], tile_cols[i]) are all different. `tile_cols`: pairs with tile_rows as above.
All inputs are finite; a program needn't handle non-finite values.
Results may differ from a plain program's by a relative error of at most 0.0049.
Values may be sent and summed in bfloat16 or wider, within the bound.
A program may use at most 256 MiB of HBM per device.

v0:
```python
import jax
import jax.numpy as jnp
from jax import lax
from jax.sharding import PartitionSpec as P


def shards(tokens, gain, tiles, tile_rows, tile_cols, cotangent):
    count = tokens.shape[0]
    width = tokens.shape[1]
    tile = tiles.shape[1]
    row_blocks = width // tile
    col_blocks = cotangent.shape[1] // tile
    x32 = tokens.astype(jnp.float32)
    scale = lax.rsqrt(jnp.mean(x32 * x32, axis=-1, keepdims=True) + 1e-05)
    normed = (x32 * scale * gain).astype(jnp.bfloat16)
    xblocks = normed.reshape(count, row_blocks, tile)
    gblocks = cotangent.reshape(count, col_blocks, tile)
    piece = lax.all_gather(tiles, "fsdp", axis=0, tiled=True)
    rows = tile_rows
    cols = tile_cols
    xsel = jnp.take(xblocks, rows, axis=1)
    gsel = jnp.take(gblocks, cols, axis=1)
    forward = jnp.einsum("tkj,kjm->tkm", xsel, piece, preferred_element_type=jnp.float32)
    backward = jnp.einsum("tkm,kjm->tkj", gsel, piece, preferred_element_type=jnp.float32)
    stacked = jnp.stack([forward, backward], axis=0)
    outsum = jnp.zeros((count, col_blocks, tile), jnp.float32).at[:, tile_cols].add(stacked[0])
    back = jnp.zeros((count, row_blocks, tile), jnp.float32).at[:, tile_rows].add(stacked[1])
    projected = outsum.reshape(count, col_blocks * tile).astype(jnp.bfloat16)
    dnormed = back.reshape(count, width)
    gain_grad = lax.psum(jnp.sum(dnormed * x32 * scale, axis=0), ("fsdp", "dp"))
    inner = jnp.mean(x32 * gain * dnormed, axis=-1, keepdims=True)
    token_grad = (scale * gain * dnormed - x32 * scale**3 * inner).astype(jnp.bfloat16)
    group = tiles.shape[0]
    number = tiles.shape[0] * lax.axis_size("fsdp")

    def group_terms(first):
        rows = lax.dynamic_slice_in_dim(tile_rows, first, group, 0)
        cols = lax.dynamic_slice_in_dim(tile_cols, first, group, 0)
        xsel = jnp.take(xblocks, rows, axis=1)
        gsel = jnp.take(gblocks, cols, axis=1)
        return jnp.einsum("tkj,tkm->kjm", xsel, gsel, preferred_element_type=jnp.float32)

    firsts = group * jnp.arange(number // group, dtype=jnp.int32)
    result = lax.map(group_terms, firsts)
    owned = lax.psum_scatter(
        result.reshape(number, tile, tile), "fsdp", scatter_dimension=0, tiled=True
    )
    tile_grad = lax.psum(owned, "dp")
    return (projected, token_grad, tile_grad, gain_grad)


def solution(mesh):
    placed = (
        P(("fsdp", "dp"), None),
        P(),
        P("fsdp", None, None),
        P(),
        P(),
        P(("fsdp", "dp"), None),
    )
    return jax.shard_map(
        shards,
        mesh=mesh,
        in_specs=placed,
        out_specs=(P(("fsdp", "dp"), None), P(("fsdp", "dp"), None), P("fsdp", None, None), P()),
        check_vma=False,
    )
```

profile of v0, /device:TPU:0, one launch (start us, length us, event | category | flops | bytes accessed | tf_op | source)
XLA Modules:
  0.0 432.9 jit_solution(535753344430040512)
XLA Ops:
  7.2 0.7 all-gather.2.cloned.1.call-update
  8.0 6.1 %copy.35 = bf16[128,14336]{0,1:T(8,128)(2,1)} copy(bf16[128,14336]{1,0:T(8,128)(2,1)} %param.13) | data formatting | bytes 7340032 | tf_op args[5]
  14.0 6.1 %copy.36 = bf16[128,112,128]{2,0,1:T(8,128)(2,1)} copy(bf16[128,112,128]{0,2,1:T(8,128)(2,1)} %bitcast.38) | data formatting | bytes 7340032 | tf_op jit(solution)/shard_map/reshape | solution.py:17
  20.1 0.7 copy.32
  20.8 5.3 %gather_fusion.3 = bf16[128,128,128]{2,1,0:T(8,128)(2,1)} fusion(bf16[128,112,128]{2,0,1:T(8,128)(2,1)} %copy.36, s32[1024]{0:T(1024)S(1)} %pad_clamp_fusion.2), kind=kCustom, calls=%fused_computation.3 | custom fusion | bytes 8389120 | tf_op jit(solution)/shard_map/jit(_take)/gather | solution.py:22
  26.1 0.6 fusion.17
  26.7 59.6 %all-gather.2.cloned.1.call-done = bf16[128,128,128]{2,1,0:T(8,128)(2,1)} async-done(((bf16[16,128,128]{2,1,0:T(8,128)(2,1)}), bf16[128,128,128]{2,1,0:T(8,128)(2,1)}) %all-gather.2.cloned.1.call-update) | async-done | bytes 4194320 | tf_op jit(solution)/shard_map/all_gather | solution.py:18
  86.3 9.8 %fusion.9 = f32[128,128,128]{2,1,0:T(8,128)} fusion(bf16[128,128,128]{2,1,0:T(8,128)(2,1)} %all-gather.2.cloned.1.call-done, bf16[128,128,128]{2,1,0:T(8,128)(2,1)} %gather_fusion.3, pred[128]{0:T(512)(128)(4,1)S(1)} %compare_and_fusion.2), kind=kOutput, calls=%fused_computation.22 | convolution fusion | flops 538968064 | bytes 16777344 | tf_op jit(solution)/shard_map/tkm,kjm->tkj/dot_general | solution.py:24
  96.0 0.2 broadcast_in_dim.69
  96.3 17.0 %scatter_fusion.1 = f32[128,32,128]{2,0,1:T(8,128)S(1)} fusion(f32[128,32,128]{2,0,1:T(8,128)S(1)} %broadcast_in_dim.69, s32[128]{0:T(128)S(1)} %compare_select_fusion.2, f32[128,128,128]{2,1,0:T(8,128)} %fusion.9), kind=kCustom, calls=%fused_computation.5 | custom fusion | flops 2097152 | bytes 25166336 | tf_op jit(solution)/shard_map/scatter-add | solution.py:27
  113.3 1.8 copy.37
  115.1 2.6 fusion.26
  117.8 1.8 fusion.22
  119.6 0.7 copy.33
  120.2 59.3 %while.10 = (s32[]{:T(128)}, f32[8,16,128,128]{3,2,1,0:T(8,128)}, s32[8]{0:T(128)S(1)}, s32[128]{0:T(128)S(1)}, bf16[128,32,128]{2,0,1:T(8,128)(2,1)S(1)}, /*ind...) while((s32[]{:T(128)}, f32[8,16,128,128]{3,2,1,0:T(8,128)}, ...), condition=%wide.region_5.6_spmd, body=%wide.region_4.5_spmd.sunk | while | flops 67635392 | bytes 4203735 | solution.py:44
  120.2 0.6 dynamic_slice.15
  122.8 0.1 compare_and_fusion.5
  122.9 2.7 gather_fusion
  125.6 0.6 gather_fusion.1
  126.2 1.4 fusion.38
  127.7 0.6 dynamic_slice.15
  130.2 0.1 compare_and_fusion.5
  130.3 2.7 gather_fusion
  133.0 0.6 gather_fusion.1
  133.6 1.5 fusion.38
  135.1 0.6 dynamic_slice.15
  137.6 0.1 compare_and_fusion.5
  137.7 2.7 gather_fusion
  140.4 0.6 gather_fusion.1
  141.1 1.4 fusion.38
  142.5 0.6 dynamic_slice.15
  145.0 0.1 compare_and_fusion.5
  145.1 2.7 gather_fusion
  147.8 0.6 gather_fusion.1
  148.5 1.4 fusion.38
  149.9 0.6 dynamic_slice.15
  152.4 0.1 compare_and_fusion.5
  152.5 2.7 gather_fusion
  155.2 0.6 gather_fusion.1
  155.9 1.4 fusion.38
  157.3 0.6 dynamic_slice.15
  159.9 2.7 gather_fusion
  162.6 0.6 gather_fusion.1
  163.3 1.4 fusion.38
  164.7 0.6 dynamic_slice.15
  167.3 2.7 gather_fusion
  170.0 0.6 gather_fusion.1
  170.7 1.4 fusion.38
  172.1 0.6 dynamic_slice.15
  174.7 2.7 gather_fusion
  177.5 0.6 gather_fusion.1
  178.1 1.4 fusion.38
  179.5 0.2 all-reduce.2.cloned.1.call-start
  179.8 3.1 gather_fusion.2
  182.9 144.1 %reduce-scatter.2.cloned.1.call-done = f32[16,128,128]{2,1,0:T(8,128)} async-done(((f32[128,128,128]{2,1,0:T(8,128)}), f32[16,128,128]{2,1,0:T(8,128)}) %reduce-scatter.2.cloned.1.call-update) | async-done | bytes 1048592 | tf_op jit(solution)/shard_map/reduce_scatter | solution.py:45
  327.0 8.0 %fusion.11 = f32[128,128,128]{2,1,0:T(8,128)} fusion(bf16[128,128,128]{2,1,0:T(8,128)(2,1)} %all-gather.2.cloned.1.call-done, bf16[128,128,128]{2,1,0:T(8,128)(2,1)} %gather_fusion.2, pred[128]{0:T(512)(128)(4,1)S(1)} %compare_and_fusion.3), kind=kOutput, calls=%fused_computation.24 | convolution fusion | flops 538968064 | bytes 16777344 | tf_op jit(solution)/shard_map/tkj,kjm->tkm/dot_general | solution.py:23
  335.0 3.9 broadcast_in_dim.64
  338.9 26.7 %scatter_fusion = f32[128,112,128]{2,0,1:T(8,128)} fusion(f32[128,112,128]{2,0,1:T(8,128)} %broadcast_in_dim.64, s32[128]{0:T(128)S(1)} %compare_select_fusion.3, f32[128,128,128]{2,1,0:T(8,128)} %fusion.11), kind=kCustom, calls=%fused_computation.4 | custom fusion | flops 2097152 | bytes 25166336 | tf_op jit(solution)/shard_map/scatter-add | solution.py:26
  365.7 5.8 %convert_element_type.17 = bf16[128,112,128]{2,0,1:T(8,128)(2,1)} convert(f32[128,112,128]{2,0,1:T(8,128)} %scatter_fusion) | non-fusion elementwise | flops 1835008 | bytes 11010048 | tf_op jit(solution)/shard_map/convert_element_type | solution.py:28
  371.4 6.1 %copy.34 = bf16[128,112,128]{0,2,1:T(8,128)(2,1)} copy(bf16[128,112,128]{2,0,1:T(8,128)(2,1)} %convert_element_type.17) | data formatting | bytes 7340032 | tf_op jit(solution)/shard_map/convert_element_type | solution.py:28
  377.5 6.2 %copy.40 = bf16[128,14336]{1,0:T(8,128)(2,1)} copy(bf16[128,14336]{0,1:T(8,128)(2,1)} %bitcast.37) | data formatting | bytes 7340032
  383.7 1.3 copy.41
  385.0 39.1 %psum.15 = f32[4096]{0:T(1024)} all-reduce(f32[4096]{0:T(1024)S(1)} %get-tuple-element.68), channel_id=1, replica_groups=mesh['fsdp'=8,'dp'=4] {'fsdp','dp'}, use_global_device_ids=true, to_apply=%region_9.10 | all-reduce | flops 4096 | bytes 32768 | tf_op jit(solution)/shard_map/psum | solution.py:30
  424.1 2.3 copy.53
  (46 shorter events, 0.5 us)
Async XLA Ops:
  7.2 79.1 %all-gather.2.cloned.1.call-start = ((), (), s32[]{:S(2)}) async-start(), calls=%async_computation.1 | async-start | bytes 4718592 | tf_op jit(solution)/shard_map/all_gather | solution.py:18
  7.9 319.1 %reduce-scatter.2.cloned.1.call-start = ((), (), s32[]{:S(2)}) async-start(), calls=%async_computation.2 | async-start | bytes 9437184 | tf_op jit(solution)/shard_map/reduce_scatter | solution.py:45
  14.0 6.1 %copy-start.2 = (bf16[128,4096]{1,0:T(8,128)(2,1)S(1)}, bf16[128,4096]{1,0:T(8,128)(2,1)}, u32[]{:S(2)}) copy-start(bf16[128,4096]{1,0:T(8,128)(2,1)} %param.8) | copy-start | bytes 3145732
  14.0 6.7 %copy-start.4 = (s32[128]{0:T(128)S(1)}, s32[128]{0:T(128)}, u32[]{:S(2)}) copy-start(s32[128]{0:T(128)} %param.12) | copy-start | bytes 1540
  20.8 5.9 %copy-start.5 = (s32[128]{0:T(128)S(1)}, s32[128]{0:T(128)}, u32[]{:S(2)}) copy-start(s32[128]{0:T(128)} %param.11) | copy-start | bytes 1540
  113.3 1.8 copy-start.3
  115.1 2.7 copy-start
  179.5 244.6 %all-reduce.2.cloned.1.call-start = ((), (), s32[]{:S(2)}) async-start(), calls=%async_computation.3 | async-start | bytes 2097152 | tf_op jit(solution)/shard_map/psum | solution.py:48
  377.5 6.2 %copy-start.1 = (bf16[128,4096]{0,1:T(8,128)(2,1)S(1)}, bf16[128,4096]{0,1:T(8,128)(2,1)}, u32[]{:S(2)}) copy-start(bf16[128,4096]{0,1:T(8,128)(2,1)} %get-tuple-element.90) | copy-start | bytes 3145732
Sparse Core Ops, SparseCore 0:
  10.1 76.0 all-gather.1
  179.7 147.2 reduce-scatter.1
  329.5 35.0 all-reduce.1
where the time goes:
time: 435 us; the launch traced here: 433 us
  waiting for transfers between devices  204 us (47%)
  local copies, waits for them, and re-layouts  74.9 us (17%)
  other arithmetic  55.3 us (13%)
  blocking collectives  39.1 us (9%)
  matrix products  29.2 us (7%)
  loops' own time  15.8 us (4%)
  between operations  13.9 us (3%)
    reduce_scatter x1, waiting for transfers between devices, shards(): lax.psum_scatter(result.reshape(number, tile, tile), 'fsdp', scatter_dime...  144 us
    all_gather x1, waiting for transfers between devices, shards(): piece = lax.all_gather(tiles, 'fsdp', axis=0, tiled=True)  59.6 us
    psum x1, blocking collectives, shards(): gain_grad = lax.psum(jnp.sum(dnormed * x32 * scale, axis=0), ('fsdp', 'dp'))  39.1 us
    scatter-add x1, other arithmetic, shards(): jnp.zeros((count, col_blocks, tile), jnp.float32).at[:, tile_cols]  26.7 us
    gather x8, local copies, waits for them, and re-layouts, group_terms(): gsel = jnp.take(gblocks, cols, axis=1)  21.5 us
    scatter-add x1, other arithmetic, shards(): jnp.zeros((count, row_blocks, tile), jnp.float32).at[:, tile_rows]  17 us
    unnamed x17, local copies, waits for them, and re-layouts  16.5 us
    another operation x1, loops' own time, shards(): result = lax.map(group_terms, firsts)  15.8 us
  transfers between devices with their start and end apart: 3, of which 2 were waited for; matrix products, arithmetic and copies ran while one was open for 18% of the time, Pallas kernels for 0%

commit v1 on v0

v1 whole, which is shorter than its diff:
```python
import functools

import jax
import jax.numpy as jnp
from jax import lax
from jax.experimental import pallas as pl
from jax.experimental.pallas import tpu as pltpu
from jax.sharding import PartitionSpec as P

MESH = pl.DeviceIdType.MESH
F32 = jnp.float32
BF16 = jnp.bfloat16
UNROLL = 8


def remote(src, dst, send, recv, f, d):
    return pltpu.make_async_remote_copy(
        src_ref=src, dst_ref=dst, send_sem=send, recv_sem=recv,
        device_id={"fsdp": f, "dp": d}, device_id_type=MESH,
    )


def row_scale(tok_ref, width, tile):
    total = jnp.zeros((tok_ref.shape[0], tile), F32)
    for b in range(width // tile):
        x = tok_ref[:, b * tile:(b + 1) * tile].astype(F32)
        total = total + x * x
    mean = jnp.sum(total, axis=-1, keepdims=True) / width
    return lax.rsqrt(mean + 1e-05)


def grads_kernel(rows_ref, cols_ref, tok_ref, gain_ref, cot_ref, part_ref, normed_t):
    number, tile = part_ref.shape[0], part_ref.shape[1]
    width = tok_ref.shape[1]
    scale = row_scale(tok_ref, width, tile)
    for b in range(width // tile):
        at = slice(b * tile, (b + 1) * tile)
        x = tok_ref[:, at].astype(F32)
        normed_t[b] = (x * scale * gain_ref[:, at]).T.astype(BF16)

    def body(i, carry):
        terms = []
        for u in range(UNROLL):
            k = i * UNROLL + u
            col = pl.multiple_of(cols_ref[k] * tile, tile)
            terms.append(jnp.dot(normed_t[rows_ref[k]], cot_ref[:, pl.ds(col, tile)], preferred_element_type=F32))
        for u in range(UNROLL):
            part_ref[i * UNROLL + u] = terms[u].astype(BF16)
        return carry

    lax.fori_loop(0, number // UNROLL, body, 0)


def comm_kernel(
    A, tiles_ref, part_ref, ag, out_ref,
    rc, ry, rz, xs, rx,
    lsem, cs, cr, ys, yr, zs, zr, xss, xrs, fs, fr,
    ays, ayr, azs, azr, axs, axr, acs, acr,
):
    f, d = lax.axis_index("fsdp"), lax.axis_index("dp")
    z, y = f // 2, f % 2
    x, c = d // 2, d % 2
    fy = z * 2 + (1 - y)
    dc = x * 2 + (1 - c)
    dx = (1 - x) * 2 + c
    dxc = (1 - x) * 2 + (1 - c)
    group = tiles_ref.shape[0]
    h, q = group // 2, group // 4
    has_left, has_right = z > 0, z < A - 1

    barrier = pltpu.get_barrier_semaphore()

    def greet(ff, dd):
        pl.semaphore_signal(barrier, inc=1, device_id={"fsdp": ff, "dp": dd}, device_id_type=MESH)

    greet(f, dc)
    greet(f, dx)
    greet(fy, d)
    pl.when(has_left)(lambda: greet(f - 2, d))
    pl.when(has_right)(lambda: greet(f + 2, d))
    pl.semaphore_wait(barrier, 3 + has_left.astype(jnp.int32) + has_right.astype(jnp.int32))

    def quarter(fb, dd):
        return ag.at[fb, pl.ds(dd * q, q)]

    def to_core(b, yy):
        fb = b * 2 + yy
        return remote(part_ref.at[fb, pl.ds((1 - c) * h, h)], rc.at[fb], cs.at[fb], cr.at[fb], f, dc)

    def to_y(b):
        return remote(rc.at[b * 2 + 1 - y], ry.at[b], ys.at[b], yr.at[b], fy, d)

    def to_right(b):
        return remote(rc.at[b * 2 + y], rz.at[b], zs.at[b], zr.at[b], f + 2, d)

    def to_left(b):
        slot = jnp.where(b == z - 1, A, b)
        return remote(rc.at[b * 2 + y], rz.at[slot], zs.at[b], zr.at[slot], f - 2, d)

    def arrived(slot):
        remote(rz.at[slot], rz.at[slot], zs.at[0], zr.at[slot], fy, d).wait_recv()

    own = tiles_ref.at[pl.ds(d * q, q)]
    own_y = remote(own, quarter(f, d), ays, ayr, fy, d)

    def ag_left(fb, src):
        return remote(src, quarter(fb, d), azs.at[0, fb], azr.at[fb], f - 2, d)

    def ag_right(fb, src):
        return remote(src, quarter(fb, d), azs.at[1, fb], azr.at[fb], f + 2, d)

    def ag_x(fb):
        return remote(quarter(fb, d), quarter(fb, d), axs.at[fb], axr.at[fb], f, dx)

    def ag_core(fb, which):
        dd = d if which == 0 else dx
        return remote(quarter(fb, dd), quarter(fb, dd), acs.at[which, fb], acr.at[which, fb], f, dc)

    def ag_landed(fb, dd, sem):
        remote(quarter(fb, dd), quarter(fb, dd), ays, sem, fy, d).wait_recv()

    def spread(fb):
        ag_x(fb).start()
        ag_core(fb, 0).start()

    own_y.start()
    pl.when(has_left)(lambda: ag_left(f, own).start())
    pl.when(has_right)(lambda: ag_right(f, own).start())
    for b in range(A):
        to_core(b, 1 - y).start()
    for b in range(A):
        to_core(b, y).start()
    keep = pltpu.make_async_copy(tiles_ref, ag.at[f], lsem)
    keep.start()

    def halves(fb):
        return part_ref[fb, pl.ds(c * h, h)].astype(F32) + rc[fb].astype(F32)

    for b in range(A):
        fb = b * 2 + 1 - y
        to_core(b, 1 - y).wait_recv()
        rc[fb] = halves(fb).astype(BF16)
        to_y(b).start()

    ag_landed(fy, d, ayr)
    pl.when(has_left)(lambda: ag_left(fy, quarter(fy, d)).start())
    pl.when(has_right)(lambda: ag_right(fy, quarter(fy, d)).start())
    spread(fy)

    def summed(b):
        to_core(b, y).wait_recv()
        to_y(b).wait_recv()
        return halves(b * 2 + y) + ry[b].astype(F32)

    def gather_from_left(s):
        b = z - s
        for yy in range(2):
            fb = b * 2 + yy
            ag_landed(fb, d, azr.at[fb])
            pl.when(has_right)(lambda: ag_right(fb, quarter(fb, d)).start())
            spread(fb)

    def gather_from_right(s):
        b = z + s
        for yy in range(2):
            fb = b * 2 + yy
            ag_landed(fb, d, azr.at[fb])
            pl.when(has_left)(lambda: ag_left(fb, quarter(fb, d)).start())
            spread(fb)

    def send_sum_right(s):
        b = z + s
        fb = b * 2 + y
        rc[fb] = summed(b).astype(BF16)

        @pl.when(has_left)
        def _():
            arrived(b)
            rc[fb] = (rc[fb].astype(F32) + rz[b].astype(F32)).astype(BF16)

        to_right(b).start()

    def send_sum_left(s):
        b = z - s
        fb = b * 2 + y
        rc[fb] = summed(b).astype(BF16)

        @pl.when(has_right)
        def _():
            arrived(b)
            rc[fb] = (rc[fb].astype(F32) + rz[b].astype(F32)).astype(BF16)

        to_left(b).start()

    for s in range(1, A):
        far = A - s
        pl.when(z + far < A)(functools.partial(send_sum_right, far))
        pl.when(z - far >= 0)(functools.partial(send_sum_left, far))
        pl.when(z - s >= 0)(functools.partial(gather_from_left, s))
        pl.when(z + s < A)(functools.partial(gather_from_right, s))

    mine = pl.ds(c * h, h)
    out_ref[mine] = summed(z)

    @pl.when(has_left)
    def _():
        arrived(z)
        out_ref[mine] = out_ref[mine] + rz[z].astype(F32)

    @pl.when(has_right)
    def _():
        arrived(A)
        out_ref[mine] = out_ref[mine] + rz[A].astype(F32)

    xs[...] = out_ref[mine].astype(BF16)
    across = remote(xs, rx, xss, xrs, f, dx)
    across.start()

    def visit(fn):
        fn(fy)
        for s in range(1, A):
            @pl.when(z - s >= 0)
            def _():
                fn((z - s) * 2)
                fn((z - s) * 2 + 1)

            @pl.when(z + s < A)
            def _():
                fn((z + s) * 2)
                fn((z + s) * 2 + 1)

    def relay(fb):
        ag_landed(fb, dx, axr.at[fb])
        ag_core(fb, 1).start()

    visit(relay)

    across.wait_recv()
    out_ref[mine] = xs[...].astype(F32) + rx[...].astype(F32)
    last = remote(out_ref.at[mine], out_ref.at[mine], fs, fr, f, dc)
    last.start()

    def finish(fb):
        ag_landed(fb, dc, acr.at[0, fb])
        ag_landed(fb, dxc, acr.at[1, fb])
        ag_x(fb).wait_send()
        ag_core(fb, 0).wait_send()
        ag_core(fb, 1).wait_send()

    visit(finish)

    other = out_ref.at[pl.ds((1 - c) * h, h)]
    remote(other, other, fs, fr, f, dc).wait_recv()
    last.wait_send()
    across.wait_send()
    keep.wait()
    own_y.wait_send()
    for fb in (f, fy):
        pl.when(has_left)(lambda: ag_left(fb, own).wait_send())
        pl.when(has_right)(lambda: ag_right(fb, own).wait_send())
    for b in range(A):
        to_core(b, 0).wait_send()
        to_core(b, 1).wait_send()
        to_y(b).wait_send()
    for s in range(1, A):
        @pl.when(z + s < A)
        def _():
            to_right(z + s).wait_send()
            for yy in range(2):
                pl.when(has_left)(lambda: ag_left((z + s) * 2 + yy, own).wait_send())

        @pl.when(z - s >= 0)
        def _():
            to_left(z - s).wait_send()
            for yy in range(2):
                pl.when(has_right)(lambda: ag_right((z - s) * 2 + yy, own).wait_send())


def apply_kernel(
    rows_ref, cols_ref, tok_ref, gain_ref, tiles_ref, cot_ref, proj_ref, tgrad_ref, ggrad_ref,
    normed, outsum, back,
):
    number, tile = tiles_ref.shape[0], tiles_ref.shape[1]
    count, width = tok_ref.shape
    scale = row_scale(tok_ref, width, tile)
    for b in range(width // tile):
        at = slice(b * tile, (b + 1) * tile)
        normed[b] = (tok_ref[:, at].astype(F32) * scale * gain_ref[:, at]).astype(BF16)
        back[b] = jnp.zeros((count, tile), F32)

    def clear(b, carry):
        outsum[b] = jnp.zeros((count, tile), F32)
        return carry

    lax.fori_loop(0, outsum.shape[0], clear, 0)

    def body(i, carry):
        forward, backward, places = [], [], []
        for u in range(UNROLL):
            k = i * UNROLL + u
            r, c = rows_ref[k], cols_ref[k]
            places.append((r, c))
            weight = tiles_ref[k]
            g = cot_ref[:, pl.ds(pl.multiple_of(c * tile, tile), tile)]
            forward.append(jnp.dot(normed[r], weight, preferred_element_type=F32))
            backward.append(lax.dot_general(g, weight, (((1,), (1,)), ((), ())), preferred_element_type=F32))
        for u in range(UNROLL):
            r, c = places[u]
            outsum[c] = outsum[c] + forward[u]
            back[r] = back[r] + backward[u]
        return carry

    lax.fori_loop(0, number // UNROLL, body, 0)

    inner = jnp.zeros((count, tile), F32)
    for b in range(width // tile):
        at = slice(b * tile, (b + 1) * tile)
        x = tok_ref[:, at].astype(F32)
        dn = back[b]
        inner = inner + x * gain_ref[:, at] * dn
        ggrad_ref[b:b + 1, :] = jnp.sum(dn * x * scale, axis=0, keepdims=True)
    inner = jnp.sum(inner, axis=-1, keepdims=True) / width
    weight = scale * scale * scale * inner
    for b in range(width // tile):
        at = slice(b * tile, (b + 1) * tile)
        x = tok_ref[:, at].astype(F32)
        tgrad_ref[:, at] = (scale * gain_ref[:, at] * back[b] - x * weight).astype(BF16)
    for b in range(outsum.shape[0]):
        proj_ref[:, b * tile:(b + 1) * tile] = outsum[b].astype(BF16)


def gain_kernel(steps, part_ref, out_ref, acc, got, ssem, rsem):
    f, d = lax.axis_index("fsdp"), lax.axis_index("dp")

    def partner(step):
        axis, bit = step
        me = f if axis == "fsdp" else d
        there = me + bit - 2 * bit * ((me // bit) % 2)
        return (there, d) if axis == "fsdp" else (f, there)

    barrier = pltpu.get_barrier_semaphore()
    for step in steps:
        ff, dd = partner(step)
        pl.semaphore_signal(barrier, inc=1, device_id={"fsdp": ff, "dp": dd}, device_id_type=MESH)
    pl.semaphore_wait(barrier, len(steps))
    acc[0] = part_ref[...]
    for i, step in enumerate(steps):
        ff, dd = partner(step)
        copy = remote(acc.at[i], got.at[i], ssem.at[i], rsem.at[i], ff, dd)
        copy.start()
        copy.wait()
        acc[i + 1] = acc[i] + got[i]
    out_ref[...] = acc[len(steps)]


def bits(axis, size):
    found, bit = [], 1
    while bit < size:
        found.append((axis, bit))
        bit *= 2
    return found


def solution(mesh):
    nf, nd = mesh.shape["fsdp"], mesh.shape["dp"]
    A = nf // 2
    steps = bits("dp", nd) + bits("fsdp", nf)
    vmem = pl.BlockSpec(memory_space=pltpu.VMEM)
    smem = pl.BlockSpec(memory_space=pltpu.SMEM)
    anywhere = pl.BlockSpec(memory_space=pl.ANY)
    dma = pltpu.SemaphoreType.DMA
    params = functools.partial(pltpu.CompilerParams, vmem_limit_bytes=60 * 2**20)

    def shards(tokens, gain, tiles, tile_rows, tile_cols, cotangent):
        count, width = tokens.shape
        group, tile, _ = tiles.shape
        number = group * nf
        rb, cb = width // tile, cotangent.shape[1] // tile
        h = group // 2
        gain2 = gain.reshape(1, width)

        part = pl.pallas_call(
            grads_kernel,
            out_shape=jax.ShapeDtypeStruct((number, tile, tile), BF16),
            in_specs=[smem, smem, vmem, vmem, vmem],
            out_specs=vmem,
            scratch_shapes=[pltpu.VMEM((rb, tile, count), BF16)],
            compiler_params=params(),
        )(tile_rows, tile_cols, tokens, gain2, cotangent)

        gathered, tile_grad = pl.pallas_call(
            functools.partial(comm_kernel, A),
            out_shape=(
                jax.ShapeDtypeStruct((nf, group, tile, tile), BF16),
                jax.ShapeDtypeStruct((group, tile, tile), F32),
            ),
            in_specs=[anywhere, vmem],
            out_specs=(anywhere, vmem),
            scratch_shapes=[
                pltpu.VMEM((nf, h, tile, tile), BF16),
                pltpu.VMEM((A, h, tile, tile), BF16),
                pltpu.VMEM((A + 1, h, tile, tile), BF16),
                pltpu.VMEM((h, tile, tile), BF16),
                pltpu.VMEM((h, tile, tile), BF16),
                dma,
                dma((nf,)), dma((nf,)),
                dma((A,)), dma((A,)),
                dma((A,)), dma((A + 1,)),
                dma, dma, dma, dma,
                dma, dma,
                dma((2, nf)), dma((nf,)),
                dma((nf,)), dma((nf,)),
                dma((2, nf)), dma((2, nf)),
            ],
            compiler_params=params(collective_id=0, has_side_effects=True),
        )(tiles, part.reshape(nf, group, tile, tile))

        projected, token_grad, gain_part = pl.pallas_call(
            apply_kernel,
            out_shape=(
                jax.ShapeDtypeStruct(cotangent.shape, BF16),
                jax.ShapeDtypeStruct(tokens.shape, BF16),
                jax.ShapeDtypeStruct((rb, tile), F32),
            ),
            in_specs=[smem, smem, vmem, vmem, vmem, vmem],
            out_specs=(vmem, vmem, vmem),
            scratch_shapes=[
                pltpu.VMEM((rb, count, tile), BF16),
                pltpu.VMEM((cb, count, tile), F32),
                pltpu.VMEM((rb, count, tile), F32),
            ],
            compiler_params=params(),
        )(tile_rows, tile_cols, tokens, gain2, gathered.reshape(number, tile, tile), cotangent)

        gain_grad = pl.pallas_call(
            functools.partial(gain_kernel, steps),
            out_shape=jax.ShapeDtypeStruct((rb, tile), F32),
            in_specs=[vmem],
            out_specs=vmem,
            scratch_shapes=[
                pltpu.VMEM((len(steps) + 1, rb, tile), F32),
                pltpu.VMEM((len(steps), rb, tile), F32),
                dma((len(steps),)), dma((len(steps),)),
            ],
            compiler_params=params(collective_id=1, has_side_effects=True),
        )(gain_part)
        return (projected, token_grad, tile_grad, gain_grad.reshape(width))

    data = P(("fsdp", "dp"), None)
    return jax.shard_map(
        shards,
        mesh=mesh,
        in_specs=(data, P(), P("fsdp", None, None), P(), P(), data),
        out_specs=(data, data, P("fsdp", None, None), P()),
        check_vma=False,
    )
```

time: 435 us -> 104 us (0.24)
  waiting for transfers between devices: 204 us -> 0 us
  Pallas kernels: 0 us -> 101 us
  local copies, waits for them, and re-layouts: 74.9 us -> 2.3 us
  other arithmetic: 55.3 us -> 0 us
  blocking collectives: 39.1 us -> 0 us
  matrix products: 29.2 us -> 0 us
  loops' own time: 15.8 us -> 0 us
  between operations: 13.9 us -> 0.66 us
    reduce_scatter x1 -> x0, waiting for transfers between devices: 144 us -> none  [shards(): lax.psum_scatter(result.reshape(number, tile, tile), 'fsdp', scatter_dime...]
    pallas_call x0 -> x4, Pallas kernels: none -> 101 us  [the longest x1 61.8 us: shards(): pl.pallas_call(functools.partial(comm_kernel, A), out_shape=(jax.ShapeDty...]
    all_gather x1 -> x0, waiting for transfers between devices: 59.6 us -> none  [shards(): piece = lax.all_gather(tiles, 'fsdp', axis=0, tiled=True)]
    scatter-add x2 -> x0, other arithmetic: 43.8 us -> none  [the longest x1 26.7 us: shards(): jnp.zeros((count, col_blocks, tile), jnp.float32).at[:, tile_cols]]
    psum x1 -> x0, blocking collectives: 39.1 us -> none  [shards(): gain_grad = lax.psum(jnp.sum(dnormed * x32 * scale, axis=0), ('fsdp', 'dp'))]
    gather x18 -> x0, local copies, waits for them, and re-layouts: 35 us -> none  [the longest x8 21.5 us: group_terms(): gsel = jnp.take(gblocks, cols, axis=1)]
    dot_general x10 -> x0, matrix products: 29.2 us -> none  [the longest x8 11.4 us: group_terms(): jnp.einsum('tkj,tkm->kjm', xsel, gsel, preferred_element_type=jnp.float32)]
    another operation x1 -> x0, loops' own time: 15.8 us -> none  [shards(): result = lax.map(group_terms, firsts)]
  transfers between devices with their start and end apart: 3 -> 0, of which waited for: 2 -> 0; matrix products, arithmetic and copies ran while one was open for 18% -> 0% of each run, Pallas kernels for 0% -> 0%
where the time goes in v1:
time: 104 us
  Pallas kernels  101 us (97%)
  local copies, waits for them, and re-layouts  2.3 us (2%)
    pallas_call x1, Pallas kernels, shards(): pl.pallas_call(functools.partial(comm_kernel, A), out_shape=(jax.ShapeDty...  61.8 us
    pallas_call x1, Pallas kernels, shards(): pl.pallas_call(apply_kernel, out_shape=(jax.ShapeDtypeStruct(cotangent.sh...  15.6 us
    pallas_call x1, Pallas kernels, shards(): pl.pallas_call(functools.partial(gain_kernel, steps), out_shape=jax.Shape...  14.9 us
    pallas_call x1, Pallas kernels, shards(): pl.pallas_call(grads_kernel, out_shape=jax.ShapeDtypeStruct((number, tile...  8.69 us
    unnamed x4, local copies, waits for them, and re-layouts  2.3 us

profile of v1, /device:TPU:0, one launch (start us, length us, event | category | flops | bytes accessed | tf_op | source)
XLA Modules:
  0.0 103.9 jit_solution(4206783986207878009)
XLA Ops:
  0.6 8.7 %shard_map.93 = bf16[128,128,128]{2,1,0:T(8,128)(2,1)} custom-call(s32[128]{0:T(128)} %rows_ref.3, s32[128]{0:T(128)} %cols_ref.3, bf16[128,4096]{1,0:T(8,128)(2,1)} %tok_ref.3, f32[1,4096]{1,0:T(1,128)} %bitcast.6, bf16[128,14336]{1,0:T(8,128)(2,1)} %cot_ref.3), custom_call_target="tpu_custom_call" | custom-call | tf_op jit(solution)/shard_map/pallas_call | solution.py:382
  9.3 61.8 %shard_map.94 = (bf16[8,16,128,128]{3,2,1,0:T(8,128)(2,1)}, f32[16,128,128]{2,1,0:T(8,128)}) custom-call(bf16[16,128,128]{2,1,0:T(8,128)(2,1)} %tiles_ref.1, bf16[8,16,128,128]{3,2,1,0:T(8,128)(2,1)} %bitcast.4), custom_call_target="tpu_custom_call" | custom-call | tf_op jit(solution)/shard_map/pallas_call | solution.py:391
  71.2 0.0 copy-start
  71.2 15.6 %shard_map.95 = (bf16[128,14336]{1,0:T(8,128)(2,1)}, bf16[128,4096]{1,0:T(8,128)(2,1)}, f32[32,128]{1,0:T(8,128)}) custom-call(s32[128]{0:T(128)} %rows_ref.3, s32[128]{0:T(128)} %cols_ref.3, bf16[128,4096]{1,0:T(8,128)(2,1)} %tok_ref.3, f32[1,4096]{1,0:T(1,128)} %bitcast.7, bf16[128,128,128]{2,1,0:T(8,128)(2,1)} %bitcast.5, bf16[128,14336]{1,0:T(8,128)(2,1)} %cot_ref.3), custom_call_target="tpu_custom_call" | custom-call | tf_op jit(solution)/shard_map/pallas_call | solution.py:418
  86.7 14.9 %shard_map.96 = f32[32,128]{1,0:T(8,128)} custom-call(f32[32,128]{1,0:T(8,128)} %get-tuple-element.13.part_ref), custom_call_target="tpu_custom_call" | custom-call | tf_op jit(solution)/shard_map/pallas_call | solution.py:435
  101.6 0.0 copy-done
  101.6 1.0 copy.12
  102.6 1.3 %copy.13 = f32[4096]{0:T(1024)} copy(f32[4096]{0:T(1024)} %bitcast.8) | data formatting | bytes 32768
Async XLA Ops:
  71.2 30.5 %copy-start = (f32[16,128,128]{2,1,0:T(8,128)S(1)}, f32[16,128,128]{2,1,0:T(8,128)}, u32[]{:S(2)}) copy-start(f32[16,128,128]{2,1,0:T(8,128)} %get-tuple-element.20) | copy-start | bytes 3145732

commit v2 on v1

--- a/solution.py
+++ b/solution.py
@@ -126,26 +126,40 @@
     own_y.start()
     pl.when(has_left)(lambda: ag_left(f, own).start())
     pl.when(has_right)(lambda: ag_right(f, own).start())
-    for b in range(A):
-        to_core(b, 1 - y).start()
-    for b in range(A):
-        to_core(b, y).start()
     keep = pltpu.make_async_copy(tiles_ref, ag.at[f], lsem)
     keep.start()
 
+    after, before = A - 1 - z, z
+    more_after = after >= before
+    alone = jnp.where(more_after, after - before, before - after)
+    paired = jnp.where(more_after, before, after)
+
+    def order(i):
+        j = i - alone
+        step = paired - j // 2
+        pair = jnp.where(j % 2 == 0, z + step, z - step)
+        return jnp.where(i < alone, jnp.where(more_after, A - 1 - i, i), pair)
+
     def halves(fb):
         return part_ref[fb, pl.ds(c * h, h)].astype(F32) + rc[fb].astype(F32)
 
-    for b in range(A):
+    def give_y(b):
         fb = b * 2 + 1 - y
         to_core(b, 1 - y).wait_recv()
         rc[fb] = halves(fb).astype(BF16)
         to_y(b).start()
 
-    ag_landed(fy, d, ayr)
-    pl.when(has_left)(lambda: ag_left(fy, quarter(fy, d)).start())
-    pl.when(has_right)(lambda: ag_right(fy, quarter(fy, d)).start())
-    spread(fy)
+    for i in range(A):
+        to_core(order(i), 1 - y).start()
+    for i in range(A):
+        to_core(order(i), y).start()
+    for i in range(A):
+        give_y(order(i))
+        if i == 0:
+            ag_landed(fy, d, ayr)
+            pl.when(has_left)(lambda: ag_left(fy, quarter(fy, d)).start())
+            pl.when(has_right)(lambda: ag_right(fy, quarter(fy, d)).start())
+            spread(fy)
 
     def summed(b):
         to_core(b, y).wait_recv()
@@ -192,12 +206,17 @@
 
         to_left(b).start()
 
+    def gather(s):
+        if s < A:
+            pl.when(z - s >= 0)(functools.partial(gather_from_left, s))
+            pl.when(z + s < A)(functools.partial(gather_from_right, s))
+
+    gather(1)
     for s in range(1, A):
         far = A - s
+        gather(s + 1)
         pl.when(z + far < A)(functools.partial(send_sum_right, far))
         pl.when(z - far >= 0)(functools.partial(send_sum_left, far))
-        pl.when(z - s >= 0)(functools.partial(gather_from_left, s))
-        pl.when(z + s < A)(functools.partial(gather_from_right, s))
 
     mine = pl.ds(c * h, h)
     out_ref[mine] = summed(z)
@@ -329,42 +348,37 @@
         proj_ref[:, b * tile:(b + 1) * tile] = outsum[b].astype(BF16)
 
 
-def gain_kernel(steps, part_ref, out_ref, acc, got, ssem, rsem):
+def gain_kernel(nf, nd, part_ref, out_ref, got_d, got_f, send_d, recv_d, send_f, recv_f):
     f, d = lax.axis_index("fsdp"), lax.axis_index("dp")
-
-    def partner(step):
-        axis, bit = step
-        me = f if axis == "fsdp" else d
-        there = me + bit - 2 * bit * ((me // bit) % 2)
-        return (there, d) if axis == "fsdp" else (f, there)
-
     barrier = pltpu.get_barrier_semaphore()
-    for step in steps:
-        ff, dd = partner(step)
-        pl.semaphore_signal(barrier, inc=1, device_id={"fsdp": ff, "dp": dd}, device_id_type=MESH)
-    pl.semaphore_wait(barrier, len(steps))
-    acc[0] = part_ref[...]
-    for i, step in enumerate(steps):
-        ff, dd = partner(step)
-        copy = remote(acc.at[i], got.at[i], ssem.at[i], rsem.at[i], ff, dd)
-        copy.start()
-        copy.wait()
-        acc[i + 1] = acc[i] + got[i]
-    out_ref[...] = acc[len(steps)]
-
-
-def bits(axis, size):
-    found, bit = [], 1
-    while bit < size:
-        found.append((axis, bit))
-        bit *= 2
-    return found
+    for o in range(1, nd):
+        pl.semaphore_signal(barrier, inc=1, device_id={"fsdp": f, "dp": (d + o) % nd}, device_id_type=MESH)
+    for o in range(1, nf):
+        pl.semaphore_signal(barrier, inc=1, device_id={"fsdp": (f + o) % nf, "dp": d}, device_id_type=MESH)
+    pl.semaphore_wait(barrier, nd - 1 + nf - 1)
+
+    def exchange(n, me, got, send, recv, place):
+        out = [remote(got.at[me], got.at[me], send.at[o], recv.at[me], *place((me + o) % n)) for o in range(1, n)]
+        for copy in out:
+            copy.start()
+        for o in range(1, n):
+            there = (me + o) % n
+            remote(got.at[there], got.at[there], send.at[o], recv.at[there], *place(there)).wait_recv()
+        total = got[0]
+        for k in range(1, n):
+            total = total + got[k]
+        for copy in out:
+            copy.wait_send()
+        return total
+
+    got_d[d] = part_ref[...]
+    got_f[f] = exchange(nd, d, got_d, send_d, recv_d, lambda dd: (f, dd))
+    out_ref[...] = exchange(nf, f, got_f, send_f, recv_f, lambda ff: (ff, d))
 
 
 def solution(mesh):
     nf, nd = mesh.shape["fsdp"], mesh.shape["dp"]
     A = nf // 2
-    steps = bits("dp", nd) + bits("fsdp", nf)
     vmem = pl.BlockSpec(memory_space=pltpu.VMEM)
     smem = pl.BlockSpec(memory_space=pltpu.SMEM)
     anywhere = pl.BlockSpec(memory_space=pl.ANY)
@@ -433,14 +447,14 @@
         )(tile_rows, tile_cols, tokens, gain2, gathered.reshape(number, tile, tile), cotangent)
 
         gain_grad = pl.pallas_call(
-            functools.partial(gain_kernel, steps),
+            functools.partial(gain_kernel, nf, nd),
             out_shape=jax.ShapeDtypeStruct((rb, tile), F32),
             in_specs=[vmem],
             out_specs=vmem,
             scratch_shapes=[
-                pltpu.VMEM((len(steps) + 1, rb, tile), F32),
-                pltpu.VMEM((len(steps), rb, tile), F32),
-                dma((len(steps),)), dma((len(steps),)),
+                pltpu.VMEM((nd, rb, tile), F32),
+                pltpu.VMEM((nf, rb, tile), F32),
+                dma((nd,)), dma((nd,)), dma((nf,)), dma((nf,)),
             ],
             compiler_params=params(collective_id=1, has_side_effects=True),
         )(gain_part)

time: 104 us -> 92.3 us (0.89)
  Pallas kernels: 101 us -> 89.1 us
    pallas_call x1, Pallas kernels: 61.8 us -> 54.3 us  [shards(): pl.pallas_call(functools.partial(comm_kernel, A), out_shape=(jax.ShapeDty...]
    pallas_call x1, Pallas kernels: 14.9 us -> 10.5 us  [shards(): pl.pallas_call(functools.partial(gain_kernel, nf, nd), out_shape=jax.Shap...]
where the time goes in v2:
time: 92.3 us; the launch traced here: 92 us
  Pallas kernels  89.1 us (97%)
  local copies, waits for them, and re-layouts  2.3 us (2%)
    pallas_call x1, Pallas kernels, shards(): pl.pallas_call(functools.partial(comm_kernel, A), out_shape=(jax.ShapeDty...  54.3 us
    pallas_call x1, Pallas kernels, shards(): pl.pallas_call(apply_kernel, out_shape=(jax.ShapeDtypeStruct(cotangent.sh...  15.5 us
    pallas_call x1, Pallas kernels, shards(): pl.pallas_call(functools.partial(gain_kernel, nf, nd), out_shape=jax.Shap...  10.5 us
    pallas_call x1, Pallas kernels, shards(): pl.pallas_call(grads_kernel, out_shape=jax.ShapeDtypeStruct((number, tile...  8.68 us
    unnamed x4, local copies, waits for them, and re-layouts  2.3 us

profile of v2, /device:TPU:0, one launch (start us, length us, event | category | flops | bytes accessed | tf_op | source)
XLA Modules:
  0.0 92.0 jit_solution(13370853999561513952)
XLA Ops:
  0.6 8.7 %shard_map.93 = bf16[128,128,128]{2,1,0:T(8,128)(2,1)} custom-call(s32[128]{0:T(128)} %rows_ref.3, s32[128]{0:T(128)} %cols_ref.3, bf16[128,4096]{1,0:T(8,128)(2,1)} %tok_ref.3, f32[1,4096]{1,0:T(1,128)} %bitcast.6, bf16[128,14336]{1,0:T(8,128)(2,1)} %cot_ref.3), custom_call_target="tpu_custom_call" | custom-call | tf_op jit(solution)/shard_map/pallas_call | solution.py:396
  9.3 54.3 %shard_map.94 = (bf16[8,16,128,128]{3,2,1,0:T(8,128)(2,1)}, f32[16,128,128]{2,1,0:T(8,128)}) custom-call(bf16[16,128,128]{2,1,0:T(8,128)(2,1)} %tiles_ref.1, bf16[8,16,128,128]{3,2,1,0:T(8,128)(2,1)} %bitcast.4), custom_call_target="tpu_custom_call" | custom-call | tf_op jit(solution)/shard_map/pallas_call | solution.py:405
  63.7 0.0 copy-start
  63.7 15.5 %shard_map.95 = (bf16[128,14336]{1,0:T(8,128)(2,1)}, bf16[128,4096]{1,0:T(8,128)(2,1)}, f32[32,128]{1,0:T(8,128)}) custom-call(s32[128]{0:T(128)} %rows_ref.3, s32[128]{0:T(128)} %cols_ref.3, bf16[128,4096]{1,0:T(8,128)(2,1)} %tok_ref.3, f32[1,4096]{1,0:T(1,128)} %bitcast.7, bf16[128,128,128]{2,1,0:T(8,128)(2,1)} %bitcast.5, bf16[128,14336]{1,0:T(8,128)(2,1)} %cot_ref.3), custom_call_target="tpu_custom_call" | custom-call | tf_op jit(solution)/shard_map/pallas_call | solution.py:432
  79.2 10.5 %shard_map.96 = f32[32,128]{1,0:T(8,128)} custom-call(f32[32,128]{1,0:T(8,128)} %get-tuple-element.13.part_ref), custom_call_target="tpu_custom_call" | custom-call | tf_op jit(solution)/shard_map/pallas_call | solution.py:449
  89.7 0.0 copy-done
  89.7 1.0 %copy.12 = f32[16,128,128]{2,1,0:T(8,128)} copy(f32[16,128,128]{2,1,0:T(8,128)S(1)} %copy-done) | data formatting | bytes 2097152
  90.7 1.3 %copy.13 = f32[4096]{0:T(1024)} copy(f32[4096]{0:T(1024)} %bitcast.8) | data formatting | bytes 32768
Async XLA Ops:
  63.7 26.1 %copy-start = (f32[16,128,128]{2,1,0:T(8,128)S(1)}, f32[16,128,128]{2,1,0:T(8,128)}, u32[]{:S(2)}) copy-start(f32[16,128,128]{2,1,0:T(8,128)} %get-tuple-element.20) | copy-start | bytes 3145732

commit v3 on v2

--- a/solution.py
+++ b/solution.py
@@ -29,31 +29,9 @@
     return lax.rsqrt(mean + 1e-05)
 
 
-def grads_kernel(rows_ref, cols_ref, tok_ref, gain_ref, cot_ref, part_ref, normed_t):
-    number, tile = part_ref.shape[0], part_ref.shape[1]
-    width = tok_ref.shape[1]
-    scale = row_scale(tok_ref, width, tile)
-    for b in range(width // tile):
-        at = slice(b * tile, (b + 1) * tile)
-        x = tok_ref[:, at].astype(F32)
-        normed_t[b] = (x * scale * gain_ref[:, at]).T.astype(BF16)
-
-    def body(i, carry):
-        terms = []
-        for u in range(UNROLL):
-            k = i * UNROLL + u
-            col = pl.multiple_of(cols_ref[k] * tile, tile)
-            terms.append(jnp.dot(normed_t[rows_ref[k]], cot_ref[:, pl.ds(col, tile)], preferred_element_type=F32))
-        for u in range(UNROLL):
-            part_ref[i * UNROLL + u] = terms[u].astype(BF16)
-        return carry
-
-    lax.fori_loop(0, number // UNROLL, body, 0)
-
-
 def comm_kernel(
-    A, tiles_ref, part_ref, ag, out_ref,
-    rc, ry, rz, xs, rx,
+    A, rows_ref, cols_ref, tok_ref, gain_ref, cot_ref, tiles_ref, ag, out_ref,
+    normed_t, cot_blocks, part_ref, rc, ry, rz, xs, rx,
     lsem, cs, cr, ys, yr, zs, zr, xss, xrs, fs, fr,
     ays, ayr, azs, azr, axs, axr, acs, acr,
 ):
@@ -66,6 +44,7 @@
     dxc = (1 - x) * 2 + (1 - c)
     group = tiles_ref.shape[0]
     h, q = group // 2, group // 4
+    tile, width = tiles_ref.shape[1], tok_ref.shape[1]
     has_left, has_right = z > 0, z < A - 1
 
     barrier = pltpu.get_barrier_semaphore()
@@ -140,6 +119,29 @@
         pair = jnp.where(j % 2 == 0, z + step, z - step)
         return jnp.where(i < alone, jnp.where(more_after, A - 1 - i, i), pair)
 
+    scale = row_scale(tok_ref, width, tile)
+    for b in range(width // tile):
+        at = slice(b * tile, (b + 1) * tile)
+        normed_t[b] = (tok_ref[:, at].astype(F32) * scale * gain_ref[:, at]).T.astype(BF16)
+
+    for b in range(cot_ref.shape[1] // tile):
+        cot_blocks[b] = cot_ref[:, b * tile:(b + 1) * tile]
+
+    def terms(b, yy):
+        fb = b * 2 + yy
+
+        def body(i, carry):
+            found = []
+            for u in range(UNROLL):
+                k = fb * group + i * UNROLL + u
+                found.append(jnp.dot(normed_t[rows_ref[k]], cot_blocks[cols_ref[k]], preferred_element_type=F32))
+            for u in range(UNROLL):
+                part_ref[fb, i * UNROLL + u] = found[u].astype(BF16)
+            return carry
+
+        lax.fori_loop(0, group // UNROLL, body, 0)
+        to_core(b, yy).start()
+
     def halves(fb):
         return part_ref[fb, pl.ds(c * h, h)].astype(F32) + rc[fb].astype(F32)
 
@@ -150,16 +152,14 @@
         to_y(b).start()
 
     for i in range(A):
-        to_core(order(i), 1 - y).start()
-    for i in range(A):
-        to_core(order(i), y).start()
-    for i in range(A):
-        give_y(order(i))
+        terms(order(i), 1 - y)
         if i == 0:
             ag_landed(fy, d, ayr)
             pl.when(has_left)(lambda: ag_left(fy, quarter(fy, d)).start())
             pl.when(has_right)(lambda: ag_right(fy, quarter(fy, d)).start())
             spread(fy)
+        else:
+            give_y(order(i - 1))
 
     def summed(b):
         to_core(b, y).wait_recv()
@@ -211,7 +211,11 @@
             pl.when(z - s >= 0)(functools.partial(gather_from_left, s))
             pl.when(z + s < A)(functools.partial(gather_from_right, s))
 
+    terms(order(0), y)
+    give_y(order(A - 1))
     gather(1)
+    for i in range(1, A):
+        terms(order(i), y)
     for s in range(1, A):
         far = A - s
         gather(s + 1)
@@ -393,24 +397,18 @@
         h = group // 2
         gain2 = gain.reshape(1, width)
 
-        part = pl.pallas_call(
-            grads_kernel,
-            out_shape=jax.ShapeDtypeStruct((number, tile, tile), BF16),
-            in_specs=[smem, smem, vmem, vmem, vmem],
-            out_specs=vmem,
-            scratch_shapes=[pltpu.VMEM((rb, tile, count), BF16)],
-            compiler_params=params(),
-        )(tile_rows, tile_cols, tokens, gain2, cotangent)
-
         gathered, tile_grad = pl.pallas_call(
             functools.partial(comm_kernel, A),
             out_shape=(
                 jax.ShapeDtypeStruct((nf, group, tile, tile), BF16),
                 jax.ShapeDtypeStruct((group, tile, tile), F32),
             ),
-            in_specs=[anywhere, vmem],
+            in_specs=[smem, smem, vmem, vmem, vmem, anywhere],
             out_specs=(anywhere, vmem),
             scratch_shapes=[
+                pltpu.VMEM((rb, tile, count), BF16),
+                pltpu.VMEM((cb, count, tile), BF16),
+                pltpu.VMEM((nf, group, tile, tile), BF16),
                 pltpu.VMEM((nf, h, tile, tile), BF16),
                 pltpu.VMEM((A, h, tile, tile), BF16),
                 pltpu.VMEM((A + 1, h, tile, tile), BF16),
@@ -427,7 +425,7 @@
                 dma((2, nf)), dma((2, nf)),
             ],
             compiler_params=params(collective_id=0, has_side_effects=True),
-        )(tiles, part.reshape(nf, group, tile, tile))
+        )(tile_rows, tile_cols, tokens, gain2, cotangent, tiles)
 
         projected, token_grad, gain_part = pl.pallas_call(
             apply_kernel,

time: 92.3 us -> 80.4 us (0.87)
  Pallas kernels: 89.1 us -> 77.1 us
    pallas_call x1 -> x0, Pallas kernels: 8.68 us -> none  [shards(): pl.pallas_call(grads_kernel, out_shape=jax.ShapeDtypeStruct((number, tile...]
    pallas_call x1, Pallas kernels: 54.3 us -> 51.1 us  [shards(): pl.pallas_call(functools.partial(comm_kernel, A), out_shape=(jax.ShapeDty...]
where the time goes in v3:
time: 80.4 us; the launch traced here: 80.1 us
  Pallas kernels  77.1 us (96%)
  local copies, waits for them, and re-layouts  2.3 us (3%)
    pallas_call x1, Pallas kernels, shards(): pl.pallas_call(functools.partial(comm_kernel, A), out_shape=(jax.ShapeDty...  51.1 us
    pallas_call x1, Pallas kernels, shards(): pl.pallas_call(apply_kernel, out_shape=(jax.ShapeDtypeStruct(cotangent.sh...  15.5 us
    pallas_call x1, Pallas kernels, shards(): pl.pallas_call(functools.partial(gain_kernel, nf, nd), out_shape=jax.Shap...  10.5 us
    unnamed x4, local copies, waits for them, and re-layouts  2.3 us

profile of v3, /device:TPU:0, one launch (start us, length us, event | category | flops | bytes accessed | tf_op | source)
XLA Modules:
  0.0 80.1 jit_solution(8881025123575413843)
XLA Ops:
  0.6 51.1 %shard_map.93 = (bf16[8,16,128,128]{3,2,1,0:T(8,128)(2,1)}, f32[16,128,128]{2,1,0:T(8,128)}) custom-call(s32[128]{0:T(128)} %rows_ref.3, s32[128]{0:T(128)} %cols_ref.3, bf16[128,4096]{1,0:T(8,128)(2,1)} %tok_ref.3, f32[1,4096]{1,0:T(1,128)} %bitcast.4, bf16[128,14336]{1,0:T(8,128)(2,1)} %cot_ref.3, bf16[16,128,128]{2,1,0:T(8,128)(2,1)} %tiles_ref.1), custom_call_target="tpu_custom_call" | custom-call | tf_op jit(solution)/shard_map/pallas_call | solution.py:400
  51.7 0.0 copy-start
  51.7 15.5 %shard_map.94 = (bf16[128,14336]{1,0:T(8,128)(2,1)}, bf16[128,4096]{1,0:T(8,128)(2,1)}, f32[32,128]{1,0:T(8,128)}) custom-call(s32[128]{0:T(128)} %rows_ref.3, s32[128]{0:T(128)} %cols_ref.3, bf16[128,4096]{1,0:T(8,128)(2,1)} %tok_ref.3, f32[1,4096]{1,0:T(1,128)} %bitcast.5, bf16[128,128,128]{2,1,0:T(8,128)(2,1)} %bitcast.3, bf16[128,14336]{1,0:T(8,128)(2,1)} %cot_ref.3), custom_call_target="tpu_custom_call" | custom-call | tf_op jit(solution)/shard_map/pallas_call | solution.py:430
  67.3 10.5 %shard_map.95 = f32[32,128]{1,0:T(8,128)} custom-call(f32[32,128]{1,0:T(8,128)} %get-tuple-element.13.part_ref), custom_call_target="tpu_custom_call" | custom-call | tf_op jit(solution)/shard_map/pallas_call | solution.py:447
  77.8 0.0 copy-done
  77.8 1.0 %copy.12 = f32[16,128,128]{2,1,0:T(8,128)} copy(f32[16,128,128]{2,1,0:T(8,128)S(1)} %copy-done) | data formatting | bytes 2097152
  78.8 1.3 %copy.13 = f32[4096]{0:T(1024)} copy(f32[4096]{0:T(1024)} %bitcast.6) | data formatting | bytes 32768
Async XLA Ops:
  51.7 26.1 %copy-start = (f32[16,128,128]{2,1,0:T(8,128)S(1)}, f32[16,128,128]{2,1,0:T(8,128)}, u32[]{:S(2)}) copy-start(f32[16,128,128]{2,1,0:T(8,128)} %get-tuple-element.20) | copy-start | bytes 3145732

commit v4 on v3

--- a/solution.py
+++ b/solution.py
@@ -30,9 +30,9 @@
 
 
 def comm_kernel(
-    A, rows_ref, cols_ref, tok_ref, gain_ref, cot_ref, tiles_ref, ag, out_ref,
-    normed_t, cot_blocks, part_ref, rc, ry, rz, xs, rx,
-    lsem, cs, cr, ys, yr, zs, zr, xss, xrs, fs, fr,
+    A, rows_ref, cols_ref, tok_ref, gain_ref, cot_hbm, tiles_ref, ag, xs,
+    cot_ref, out_ref, normed_t, cot_blocks, part_ref, rc, ry, rz,
+    csem, lsem, cs, cr, ys, yr, zs, zr,
     ays, ayr, azs, azr, axs, axr, acs, acr,
 ):
     f, d = lax.axis_index("fsdp"), lax.axis_index("dp")
@@ -46,6 +46,8 @@
     h, q = group // 2, group // 4
     tile, width = tiles_ref.shape[1], tok_ref.shape[1]
     has_left, has_right = z > 0, z < A - 1
+    fetch = pltpu.make_async_copy(cot_hbm, cot_ref, csem)
+    fetch.start()
 
     barrier = pltpu.get_barrier_semaphore()
 
@@ -124,6 +126,7 @@
         at = slice(b * tile, (b + 1) * tile)
         normed_t[b] = (tok_ref[:, at].astype(F32) * scale * gain_ref[:, at]).T.astype(BF16)
 
+    fetch.wait()
     for b in range(cot_ref.shape[1] // tile):
         cot_blocks[b] = cot_ref[:, b * tile:(b + 1) * tile]
 
@@ -222,22 +225,19 @@
         pl.when(z + far < A)(functools.partial(send_sum_right, far))
         pl.when(z - far >= 0)(functools.partial(send_sum_left, far))
 
-    mine = pl.ds(c * h, h)
-    out_ref[mine] = summed(z)
+    out_ref[...] = summed(z)
 
     @pl.when(has_left)
     def _():
         arrived(z)
-        out_ref[mine] = out_ref[mine] + rz[z].astype(F32)
+        out_ref[...] = out_ref[...] + rz[z].astype(F32)
 
     @pl.when(has_right)
     def _():
         arrived(A)
-        out_ref[mine] = out_ref[mine] + rz[A].astype(F32)
-
-    xs[...] = out_ref[mine].astype(BF16)
-    across = remote(xs, rx, xss, xrs, f, dx)
-    across.start()
+        out_ref[...] = out_ref[...] + rz[A].astype(F32)
+
+    xs[...] = out_ref[...].astype(BF16)
 
     def visit(fn):
         fn(fy)
@@ -258,11 +258,6 @@
 
     visit(relay)
 
-    across.wait_recv()
-    out_ref[mine] = xs[...].astype(F32) + rx[...].astype(F32)
-    last = remote(out_ref.at[mine], out_ref.at[mine], fs, fr, f, dc)
-    last.start()
-
     def finish(fb):
         ag_landed(fb, dc, acr.at[0, fb])
         ag_landed(fb, dxc, acr.at[1, fb])
@@ -272,10 +267,6 @@
 
     visit(finish)
 
-    other = out_ref.at[pl.ds((1 - c) * h, h)]
-    remote(other, other, fs, fr, f, dc).wait_recv()
-    last.wait_send()
-    across.wait_send()
     keep.wait()
     own_y.wait_send()
     for fb in (f, fy):
@@ -300,11 +291,16 @@
 
 
 def apply_kernel(
-    rows_ref, cols_ref, tok_ref, gain_ref, tiles_ref, cot_ref, proj_ref, tgrad_ref, ggrad_ref,
-    normed, outsum, back,
+    rows_ref, cols_ref, tok_ref, gain_ref, tiles_hbm, cot_hbm, proj_hbm, tgrad_ref, ggrad_ref,
+    tiles_ref, cot_ref, proj_ref, normed, outsum, back, sems,
 ):
     number, tile = tiles_ref.shape[0], tiles_ref.shape[1]
     count, width = tok_ref.shape
+    fetch_cot = pltpu.make_async_copy(cot_hbm, cot_ref, sems.at[0])
+    fetch_tiles = pltpu.make_async_copy(tiles_hbm, tiles_ref, sems.at[1])
+    store = pltpu.make_async_copy(proj_ref, proj_hbm, sems.at[2])
+    fetch_cot.start()
+    fetch_tiles.start()
     scale = row_scale(tok_ref, width, tile)
     for b in range(width // tile):
         at = slice(b * tile, (b + 1) * tile)
@@ -316,6 +312,8 @@
         return carry
 
     lax.fori_loop(0, outsum.shape[0], clear, 0)
+    fetch_cot.wait()
+    fetch_tiles.wait()
 
     def body(i, carry):
         forward, backward, places = [], [], []
@@ -335,6 +333,9 @@
 
     lax.fori_loop(0, number // UNROLL, body, 0)
 
+    for b in range(outsum.shape[0]):
+        proj_ref[:, b * tile:(b + 1) * tile] = outsum[b].astype(BF16)
+    store.start()
     inner = jnp.zeros((count, tile), F32)
     for b in range(width // tile):
         at = slice(b * tile, (b + 1) * tile)
@@ -348,36 +349,71 @@
         at = slice(b * tile, (b + 1) * tile)
         x = tok_ref[:, at].astype(F32)
         tgrad_ref[:, at] = (scale * gain_ref[:, at] * back[b] - x * weight).astype(BF16)
-    for b in range(outsum.shape[0]):
-        proj_ref[:, b * tile:(b + 1) * tile] = outsum[b].astype(BF16)
-
-
-def gain_kernel(nf, nd, part_ref, out_ref, got_d, got_f, send_d, recv_d, send_f, recv_f):
+    store.wait()
+
+
+def finish_kernel(
+    nf, nd, part_ref, xs, gain_out, out_ref, got_d, got_f, rx, send_d, recv_d, send_f, recv_f, xss, xrs, fs, fr,
+):
     f, d = lax.axis_index("fsdp"), lax.axis_index("dp")
+    x, c = d // 2, d % 2
+    dc = x * 2 + (1 - c)
+    dx = (1 - x) * 2 + c
+    h = xs.shape[0]
+    pieces = fs.shape[0]
+    size = h // pieces
     barrier = pltpu.get_barrier_semaphore()
     for o in range(1, nd):
         pl.semaphore_signal(barrier, inc=1, device_id={"fsdp": f, "dp": (d + o) % nd}, device_id_type=MESH)
     for o in range(1, nf):
         pl.semaphore_signal(barrier, inc=1, device_id={"fsdp": (f + o) % nf, "dp": d}, device_id_type=MESH)
+    got_d[d] = part_ref[...]
     pl.semaphore_wait(barrier, nd - 1 + nf - 1)
 
-    def exchange(n, me, got, send, recv, place):
-        out = [remote(got.at[me], got.at[me], send.at[o], recv.at[me], *place((me + o) % n)) for o in range(1, n)]
-        for copy in out:
-            copy.start()
+    def copies(n, me, got, send, recv, place):
+        return [remote(got.at[me], got.at[me], send.at[o], recv.at[me], *place((me + o) % n)) for o in range(1, n)]
+
+    def total(n, me, got, send, recv, place):
         for o in range(1, n):
             there = (me + o) % n
             remote(got.at[there], got.at[there], send.at[o], recv.at[there], *place(there)).wait_recv()
-        total = got[0]
+        result = got[0]
         for k in range(1, n):
-            total = total + got[k]
-        for copy in out:
-            copy.wait_send()
-        return total
-
-    got_d[d] = part_ref[...]
-    got_f[f] = exchange(nd, d, got_d, send_d, recv_d, lambda dd: (f, dd))
-    out_ref[...] = exchange(nf, f, got_f, send_f, recv_f, lambda ff: (ff, d))
+            result = result + got[k]
+        return result
+
+    def across(p):
+        at = pl.ds(p * size, size)
+        return remote(xs.at[at], rx.at[at], xss.at[p], xrs.at[p], f, dx)
+
+    def to_core(p, core):
+        at = pl.ds(core * h + p * size, size)
+        return remote(out_ref.at[at], out_ref.at[at], fs.at[p], fr.at[p], f, dc)
+
+    replicas = (nd, d, got_d, send_d, recv_d, lambda dd: (f, dd))
+    owners = (nf, f, got_f, send_f, recv_f, lambda ff: (ff, d))
+    first = copies(*replicas)
+    for copy in first:
+        copy.start()
+    for p in range(pieces):
+        across(p).start()
+    got_f[f] = total(*replicas)
+    second = copies(*owners)
+    for copy in second:
+        copy.start()
+    for p in range(pieces):
+        across(p).wait_recv()
+        at = pl.ds(p * size, size)
+        out_ref[pl.ds(c * h + p * size, size)] = xs[at].astype(F32) + rx[at].astype(F32)
+        to_core(p, c).start()
+    gain_out[...] = total(*owners)
+    for p in range(pieces):
+        to_core(p, 1 - c).wait_recv()
+    for copy in first + second:
+        copy.wait_send()
+    for p in range(pieces):
+        across(p).wait_send()
+        to_core(p, c).wait_send()
 
 
 def solution(mesh):
@@ -397,28 +433,27 @@
         h = group // 2
         gain2 = gain.reshape(1, width)
 
-        gathered, tile_grad = pl.pallas_call(
+        gathered, summed = pl.pallas_call(
             functools.partial(comm_kernel, A),
             out_shape=(
                 jax.ShapeDtypeStruct((nf, group, tile, tile), BF16),
-                jax.ShapeDtypeStruct((group, tile, tile), F32),
+                jax.ShapeDtypeStruct((h, tile, tile), BF16),
             ),
-            in_specs=[smem, smem, vmem, vmem, vmem, anywhere],
+            in_specs=[smem, smem, vmem, vmem, anywhere, anywhere],
             out_specs=(anywhere, vmem),
             scratch_shapes=[
+                pltpu.VMEM(cotangent.shape, BF16),
+                pltpu.VMEM((h, tile, tile), F32),
                 pltpu.VMEM((rb, tile, count), BF16),
                 pltpu.VMEM((cb, count, tile), BF16),
                 pltpu.VMEM((nf, group, tile, tile), BF16),
                 pltpu.VMEM((nf, h, tile, tile), BF16),
                 pltpu.VMEM((A, h, tile, tile), BF16),
                 pltpu.VMEM((A + 1, h, tile, tile), BF16),
-                pltpu.VMEM((h, tile, tile), BF16),
-                pltpu.VMEM((h, tile, tile), BF16),
-                dma,
+                dma, dma,
                 dma((nf,)), dma((nf,)),
                 dma((A,)), dma((A,)),
                 dma((A,)), dma((A + 1,)),
-                dma, dma, dma, dma,
                 dma, dma,
                 dma((2, nf)), dma((nf,)),
                 dma((nf,)), dma((nf,)),
@@ -434,28 +469,38 @@
                 jax.ShapeDtypeStruct(tokens.shape, BF16),
                 jax.ShapeDtypeStruct((rb, tile), F32),
             ),
-            in_specs=[smem, smem, vmem, vmem, vmem, vmem],
-            out_specs=(vmem, vmem, vmem),
+            in_specs=[smem, smem, vmem, vmem, anywhere, anywhere],
+            out_specs=(anywhere, vmem, vmem),
             scratch_shapes=[
+                pltpu.VMEM((number, tile, tile), BF16),
+                pltpu.VMEM(cotangent.shape, BF16),
+                pltpu.VMEM(cotangent.shape, BF16),
                 pltpu.VMEM((rb, count, tile), BF16),
                 pltpu.VMEM((cb, count, tile), F32),
                 pltpu.VMEM((rb, count, tile), F32),
+                dma((3,)),
             ],
             compiler_params=params(),
         )(tile_rows, tile_cols, tokens, gain2, gathered.reshape(number, tile, tile), cotangent)
 
-        gain_grad = pl.pallas_call(
-            functools.partial(gain_kernel, nf, nd),
-            out_shape=jax.ShapeDtypeStruct((rb, tile), F32),
-            in_specs=[vmem],
-            out_specs=vmem,
+        pieces = 4 if h % 4 == 0 else 1
+        gain_grad, tile_grad = pl.pallas_call(
+            functools.partial(finish_kernel, nf, nd),
+            out_shape=(
+                jax.ShapeDtypeStruct((rb, tile), F32),
+                jax.ShapeDtypeStruct((group, tile, tile), F32),
+            ),
+            in_specs=[vmem, vmem],
+            out_specs=(vmem, vmem),
             scratch_shapes=[
                 pltpu.VMEM((nd, rb, tile), F32),
                 pltpu.VMEM((nf, rb, tile), F32),
+                pltpu.VMEM((h, tile, tile), BF16),
                 dma((nd,)), dma((nd,)), dma((nf,)), dma((nf,)),
+                dma((pieces,)), dma((pieces,)), dma((pieces,)), dma((pieces,)),
             ],
             compiler_params=params(collective_id=1, has_side_effects=True),
-        )(gain_part)
+        )(gain_part, summed)
         return (projected, token_grad, tile_grad, gain_grad.reshape(width))
 
     data = P(("fsdp", "dp"), None)

time: 80.4 us -> 78 us (0.970)
  Pallas kernels: 77.1 us -> 73.4 us
  local copies, waits for them, and re-layouts: 2.3 us -> 3.62 us
    pallas_call x1, Pallas kernels: 51.1 us -> 44.6 us  [shards(): pl.pallas_call(functools.partial(comm_kernel, A), out_shape=(jax.ShapeDty...]
    pallas_call x1, Pallas kernels: 10.5 us -> 13.5 us  [shards(): pl.pallas_call(functools.partial(finish_kernel, nf, nd), out_shape=(jax.S...]
    unnamed x4 -> x2, local copies, waits for them, and re-layouts: 2.3 us -> 3.62 us
where the time goes in v4:
time: 78 us; the launch traced here: 77.7 us
  Pallas kernels  73.4 us (94%)
  local copies, waits for them, and re-layouts  3.62 us (5%)
    pallas_call x1, Pallas kernels, shards(): pl.pallas_call(functools.partial(comm_kernel, A), out_shape=(jax.ShapeDty...  44.6 us
    pallas_call x1, Pallas kernels, shards(): pl.pallas_call(apply_kernel, out_shape=(jax.ShapeDtypeStruct(cotangent.sh...  15.3 us
    pallas_call x1, Pallas kernels, shards(): pl.pallas_call(functools.partial(finish_kernel, nf, nd), out_shape=(jax.S...  13.5 us
    unnamed x2, local copies, waits for them, and re-layouts  3.62 us

profile of v4, /device:TPU:0, one launch (start us, length us, event | category | flops | bytes accessed | tf_op | source)
XLA Modules:
  0.0 77.7 jit_solution(11056576406119504053)
XLA Ops:
  0.6 44.6 %shard_map.93 = (bf16[8,16,128,128]{3,2,1,0:T(8,128)(2,1)}, bf16[8,128,128]{2,1,0:T(8,128)(2,1)}) custom-call(s32[128]{0:T(128)} %rows_ref.3, s32[128]{0:T(128)} %cols_ref.3, bf16[128,4096]{1,0:T(8,128)(2,1)} %tok_ref.3, f32[1,4096]{1,0:T(1,128)} %bitcast.4, bf16[128,14336]{1,0:T(8,128)(2,1)} %cot_hbm.3, bf16[16,128,128]{2,1,0:T(8,128)(2,1)} %tiles_ref.1), custom_call_target="tpu_custom_call" | custom-call | tf_op jit(solution)/shard_map/pallas_call | solution.py:436
  45.3 15.3 %shard_map.94 = (bf16[128,14336]{1,0:T(8,128)(2,1)}, bf16[128,4096]{1,0:T(8,128)(2,1)}, f32[32,128]{1,0:T(8,128)}) custom-call(s32[128]{0:T(128)} %rows_ref.3, s32[128]{0:T(128)} %cols_ref.3, bf16[128,4096]{1,0:T(8,128)(2,1)} %tok_ref.3, f32[1,4096]{1,0:T(1,128)} %bitcast.5, bf16[128,128,128]{2,1,0:T(8,128)(2,1)} %bitcast.3, bf16[128,14336]{1,0:T(8,128)(2,1)} %cot_hbm.3), custom_call_target="tpu_custom_call" | custom-call | tf_op jit(solution)/shard_map/pallas_call | solution.py:465
  60.6 13.5 %shard_map.95 = (f32[32,128]{1,0:T(8,128)}, f32[16,128,128]{2,1,0:T(8,128)}) custom-call(f32[32,128]{1,0:T(8,128)} %get-tuple-element.14.part_ref, bf16[8,128,128]{2,1,0:T(8,128)(2,1)} %get-tuple-element.15.xs), custom_call_target="tpu_custom_call" | custom-call | tf_op jit(solution)/shard_map/pallas_call | solution.py:487
  74.0 2.3 %copy.12 = f32[16,128,128]{2,1,0:T(8,128)} copy(f32[16,128,128]{2,1,0:T(8,128)} %get-tuple-element.24) | data formatting | bytes 2097152
  76.3 1.3 %copy.13 = f32[4096]{0:T(1024)} copy(f32[4096]{0:T(1024)} %bitcast.6) | data formatting | bytes 32768

commit v5 on v4

--- a/solution.py
+++ b/solution.py
@@ -353,7 +353,7 @@
 
 
 def finish_kernel(
-    nf, nd, part_ref, xs, gain_out, out_ref, got_d, got_f, rx, send_d, recv_d, send_f, recv_f, xss, xrs, fs, fr,
+    nf, nd, part_ref, xs, gain_out, near, far, got_d, got_f, send_d, recv_d, send_f, recv_f, xss, xrs, ns, nr, fs, fr,
 ):
     f, d = lax.axis_index("fsdp"), lax.axis_index("dp")
     x, c = d // 2, d % 2
@@ -384,11 +384,14 @@
 
     def across(p):
         at = pl.ds(p * size, size)
-        return remote(xs.at[at], rx.at[at], xss.at[p], xrs.at[p], f, dx)
+        return remote(xs.at[at], far.at[pl.ds(c * h + p * size, size)], xss.at[p], xrs.at[p], f, dx)
+
+    def near_core(core):
+        return remote(xs, near.at[pl.ds(core * h, h)], ns, nr, f, dc)
 
     def to_core(p, core):
         at = pl.ds(core * h + p * size, size)
-        return remote(out_ref.at[at], out_ref.at[at], fs.at[p], fr.at[p], f, dc)
+        return remote(far.at[at], far.at[at], fs.at[p], fr.at[p], f, dc)
 
     replicas = (nd, d, got_d, send_d, recv_d, lambda dd: (f, dd))
     owners = (nf, f, got_f, send_f, recv_f, lambda ff: (ff, d))
@@ -397,18 +400,20 @@
         copy.start()
     for p in range(pieces):
         across(p).start()
+    near_core(c).start()
+    near[pl.ds(c * h, h)] = xs[...]
     got_f[f] = total(*replicas)
     second = copies(*owners)
     for copy in second:
         copy.start()
     for p in range(pieces):
         across(p).wait_recv()
-        at = pl.ds(p * size, size)
-        out_ref[pl.ds(c * h + p * size, size)] = xs[at].astype(F32) + rx[at].astype(F32)
         to_core(p, c).start()
     gain_out[...] = total(*owners)
+    near_core(1 - c).wait_recv()
     for p in range(pieces):
         to_core(p, 1 - c).wait_recv()
+    near_core(c).wait_send()
     for copy in first + second:
         copy.wait_send()
     for p in range(pieces):
@@ -484,23 +489,24 @@
         )(tile_rows, tile_cols, tokens, gain2, gathered.reshape(number, tile, tile), cotangent)
 
         pieces = 4 if h % 4 == 0 else 1
-        gain_grad, tile_grad = pl.pallas_call(
+        gain_grad, near, far = pl.pallas_call(
             functools.partial(finish_kernel, nf, nd),
             out_shape=(
                 jax.ShapeDtypeStruct((rb, tile), F32),
-                jax.ShapeDtypeStruct((group, tile, tile), F32),
+                jax.ShapeDtypeStruct((group, tile, tile), BF16),
+                jax.ShapeDtypeStruct((group, tile, tile), BF16),
             ),
             in_specs=[vmem, vmem],
-            out_specs=(vmem, vmem),
+            out_specs=(vmem, vmem, vmem),
             scratch_shapes=[
                 pltpu.VMEM((nd, rb, tile), F32),
                 pltpu.VMEM((nf, rb, tile), F32),
-                pltpu.VMEM((h, tile, tile), BF16),
                 dma((nd,)), dma((nd,)), dma((nf,)), dma((nf,)),
-                dma((pieces,)), dma((pieces,)), dma((pieces,)), dma((pieces,)),
+                dma((pieces,)), dma((pieces,)), dma, dma, dma((pieces,)), dma((pieces,)),
             ],
             compiler_params=params(collective_id=1, has_side_effects=True),
         )(gain_part, summed)
+        tile_grad = near.astype(F32) + far.astype(F32)
         return (projected, token_grad, tile_grad, gain_grad.reshape(width))
 
     data = P(("fsdp", "dp"), None)

time: 78 us -> 78 us (level)
  other arithmetic: 0 us -> 2.3 us
  local copies, waits for them, and re-layouts: 3.62 us -> 1.32 us
    add x0 -> x1, other arithmetic: none -> 2.3 us  [shards(): tile_grad = near.astype(F32) + far.astype(F32)]
    unnamed x2 -> x1, local copies, waits for them, and re-layouts: 3.62 us -> 1.32 us
where the time goes in v5:
time: 78 us; the launch traced here: 77.6 us
  Pallas kernels  73.3 us (94%)
  other arithmetic  2.3 us (3%)
  local copies, waits for them, and re-layouts  1.32 us (2%)
    pallas_call x1, Pallas kernels, shards(): pl.pallas_call(functools.partial(comm_kernel, A), out_shape=(jax.ShapeDty...  44.6 us
    pallas_call x1, Pallas kernels, shards(): pl.pallas_call(apply_kernel, out_shape=(jax.ShapeDtypeStruct(cotangent.sh...  15.3 us
    pallas_call x1, Pallas kernels, shards(): pl.pallas_call(functools.partial(finish_kernel, nf, nd), out_shape=(jax.S...  13.4 us
    add x1, other arithmetic, shards(): tile_grad = near.astype(F32) + far.astype(F32)  2.3 us

profile of v5, /device:TPU:0, one launch (start us, length us, event | category | flops | bytes accessed | tf_op | source)
XLA Modules:
  0.0 77.6 jit_solution(447898092349077106)
XLA Ops:
  0.6 44.6 %shard_map.93 = (bf16[8,16,128,128]{3,2,1,0:T(8,128)(2,1)}, bf16[8,128,128]{2,1,0:T(8,128)(2,1)}) custom-call(s32[128]{0:T(128)} %rows_ref.3, s32[128]{0:T(128)} %cols_ref.3, bf16[128,4096]{1,0:T(8,128)(2,1)} %tok_ref.3, f32[1,4096]{1,0:T(1,128)} %bitcast.4, bf16[128,14336]{1,0:T(8,128)(2,1)} %cot_hbm.3, bf16[16,128,128]{2,1,0:T(8,128)(2,1)} %tiles_ref.1), custom_call_target="tpu_custom_call" | custom-call | tf_op jit(solution)/shard_map/pallas_call | solution.py:441
  45.3 15.3 %shard_map.94 = (bf16[128,14336]{1,0:T(8,128)(2,1)}, bf16[128,4096]{1,0:T(8,128)(2,1)}, f32[32,128]{1,0:T(8,128)}) custom-call(s32[128]{0:T(128)} %rows_ref.3, s32[128]{0:T(128)} %cols_ref.3, bf16[128,4096]{1,0:T(8,128)(2,1)} %tok_ref.3, f32[1,4096]{1,0:T(1,128)} %bitcast.5, bf16[128,128,128]{2,1,0:T(8,128)(2,1)} %bitcast.3, bf16[128,14336]{1,0:T(8,128)(2,1)} %cot_hbm.3), custom_call_target="tpu_custom_call" | custom-call | tf_op jit(solution)/shard_map/pallas_call | solution.py:470
  60.6 13.4 %shard_map.95 = (f32[32,128]{1,0:T(8,128)}, bf16[16,128,128]{2,1,0:T(8,128)(2,1)}, bf16[16,128,128]{2,1,0:T(8,128)(2,1)}) custom-call(f32[32,128]{1,0:T(8,128)} %get-tuple-element.15.part_ref, bf16[8,128,128]{2,1,0:T(8,128)(2,1)} %get-tuple-element.16.xs), custom_call_target="tpu_custom_call" | custom-call | tf_op jit(solution)/shard_map/pallas_call | solution.py:492
  74.0 2.3 %convert_add_fusion = f32[16,128,128]{2,1,0:T(8,128)} fusion(bf16[16,128,128]{2,1,0:T(8,128)(2,1)} %get-tuple-element.18, bf16[16,128,128]{2,1,0:T(8,128)(2,1)} %get-tuple-element.17), kind=kLoop, calls=%fused_computation | loop fusion | flops 786432 | bytes 2097152 | tf_op jit(solution)/shard_map/add | solution.py:509
  76.3 1.3 %copy.11 = f32[4096]{0:T(1024)} copy(f32[4096]{0:T(1024)} %bitcast.6) | data formatting | bytes 32768
